TPU v7x, 128 devices: a whole 4x4x4 slice. The times are simulated.
128 devices in a mesh: gx: 4 (over x), gy: 32 (over z, y, core).
Axes of the slice: x: 4, y: 4, z: 4, core: 2. Of those that a mesh axis runs over, the one named last changes fastest.
Arguments:
- fine_feat: bfloat16 [4, 32, 16, 128, 256], P('gx', 'gy'), may hold values from -6 to 6
- coarse_grad: bfloat16 [4, 32, 4, 128, 256], P('gx', 'gy'), may hold values from -6 to 6
- kernel_map: int32 [4, 32, 27, 16], P('gx', 'gy'), may hold values from 0 to 36, as said below
- counts: int32 [4, 32], P('gx', 'gy'), may hold values from 4 to 16, as said below
- weight: bfloat16 [27, 256, 256], replicated, may hold values from -0.078125 to 0.078125
Outputs:
- fine_grad: bfloat16 [4, 32, 16, 128, 256], P('gx', 'gy')
- weight_grad: float32 [6912, 256], P(('gx', 'gy'))
Inputs may be any that keep to these rules, and one draw needn't show every extreme that they name: `kernel_map`: an entry v < 36 names coarse block v % 4 of the partition offset by (v // 4) // 3 - 1 along gx and (v // 4) % 3 - 1 along gy; 36 names no block. Entries of unoccupied slots are arbitrary. `counts`: fine block slots at or beyond a partition's count are unoccupied and their features are arbitrary.
All inputs are finite; a program needn't handle non-finite values.
Results may differ from a plain program's by a relative error of at most 0.001.
Values may be sent and summed in bfloat16 or wider, within the bound.
A program may use at most 128 MiB of HBM per device.

v0:
```python
import math

import jax
import jax.numpy as jnp
from jax import lax
from jax.sharding import PartitionSpec as P


def padded(cells, sides, width):
    for axis, dim in sides:
        count = lax.axis_size(axis)
        ends = count - 1
        head = lax.slice_in_dim(cells, 0, width, axis=dim)
        tail = lax.slice_in_dim(cells, cells.shape[dim] - width, cells.shape[dim], axis=dim)
        cells = jnp.concatenate(
            [
                lax.ppermute(tail, axis, [(i, (i + 1) % count) for i in range(ends)]),
                cells,
                lax.ppermute(head, axis, [((i + 1) % count, i) for i in range(ends)]),
            ],
            axis=dim,
        )
    return cells


def local(fine_feat, coarse_grad, kernel_map, counts, weight):
    slot_count = fine_feat.shape[2]
    block_size = fine_feat.shape[3]
    channels = fine_feat.shape[4]
    offsets = weight.shape[0]
    coarse_count = coarse_grad.shape[2]
    size_x = lax.axis_size("gx")
    size_y = lax.axis_size("gy")
    extended = padded(coarse_grad, (("gx", 0), ("gy", 1)), 1)
    coarse_pool = jnp.concatenate(
        [
            extended.reshape(9 * coarse_count, block_size, channels),
            jnp.zeros((1, block_size, channels), jnp.bfloat16),
        ],
        axis=0,
    )
    offsets_map = kernel_map[0, 0]
    occupied = (jnp.arange(slot_count, dtype=jnp.int32) < counts[0, 0]).astype(jnp.bfloat16)
    fine_rows = fine_feat[0, 0] * occupied[:, None, None]

    def offset_step(offset, carried):
        grad_acc, kernel_acc = carried
        chosen = lax.dynamic_index_in_dim(offsets_map, offset, 0, keepdims=False)
        blocks = coarse_pool[chosen]
        matrix = lax.dynamic_index_in_dim(weight, offset, 0, keepdims=False)
        grad_acc = grad_acc + jnp.einsum(
            "bvo,io->bvi", blocks, matrix, preferred_element_type=jnp.float32
        )
        kernel_piece = jnp.einsum(
            "bvi,bvo->io", fine_rows, blocks, preferred_element_type=jnp.float32
        )
        kernel_acc = lax.dynamic_update_index_in_dim(kernel_acc, kernel_piece, offset, 0)
        return (grad_acc, kernel_acc)

    starting = (
        jnp.zeros((slot_count, block_size, channels), jnp.float32),
        jnp.zeros((offsets, channels, channels), jnp.float32),
    )
    grad_in, kernel_grad = lax.fori_loop(0, offsets, offset_step, starting)
    grad_in = grad_in * occupied.astype(jnp.float32)[:, None, None]
    fine_grad = grad_in.astype(jnp.bfloat16).reshape(1, 1, slot_count, block_size, channels)
    factor = 1.0 / math.sqrt(block_size * slot_count * size_x * size_y)
    partial_sum = kernel_grad.reshape(offsets * channels, channels) * jnp.float32(factor)
    weight_grad = lax.psum_scatter(partial_sum, ("gx", "gy"), scatter_dimension=0, tiled=True)
    return (fine_grad, weight_grad)


def solution(mesh):
    return jax.shard_map(
        local,
        mesh=mesh,
        in_specs=(
            P("gx", "gy", None, None, None),
            P("gx", "gy", None, None, None),
            P("gx", "gy", None, None),
            P("gx", "gy"),
            P(),
        ),
        out_specs=(P("gx", "gy", None, None, None), P(("gx", "gy"), None)),
        check_vma=False,
    )
```

profile of v0, /device:TPU:1, one launch (start us, length us, event | category | flops | bytes accessed | tf_op | source)
XLA Modules:
  0.0 555.0 jit_solution(6817192303348278160)
XLA Ops:
  0.6 4.0 collective-permute-start
  5.9 4.0 collective-permute-done
  10.9 2.7 collective-permute-done.1
  13.6 5.0 collective-permute-start.2
  18.5 1.9 collective-permute-start.3
  21.9 2.3 bitcast_multiply_fusion
  24.3 3.2 collective-permute-done.2
  27.5 4.5 collective-permute-done.3
  35.3 143.1 %while.16 = (s32[]{:T(128)}, f32[16,128,256]{2,1,0:T(8,128)S(1)}, f32[27,256,256]{1,2,0:T(8,128)}, s32[27,16]{1,0:T(8,128)S(1)}, bf16[37,128,256]{2,1,0:T(8,128)...) while((s32[]{:T(128)}, f32[16,128,256]{2,1,0:T(8,128)S(1)}, ...), condition=%wide.region_1.2_spmd.clone, body=%wide.region_0.1_spmd.clone.sunk | while | flops 537920576 | bytes 14030215 | solution.py:64
  35.3 2.3 gather_fusion
  37.7 1.8 select_add_fusion.2
  40.6 2.3 gather_fusion
  43.0 1.8 select_add_fusion.2
  45.9 2.3 gather_fusion
  51.3 2.3 gather_fusion
  53.6 1.8 select_add_fusion.2
  56.5 2.3 gather_fusion
  58.9 1.8 select_add_fusion.2
  61.9 2.3 gather_fusion
  64.2 1.8 select_add_fusion.2
  67.2 2.3 gather_fusion
  69.5 1.8 select_add_fusion.2
  72.5 2.3 gather_fusion
  74.8 1.8 select_add_fusion.2
  77.8 2.3 gather_fusion
  80.1 1.8 select_add_fusion.2
  83.1 2.3 gather_fusion
  85.4 1.8 select_add_fusion.2
  88.4 2.3 gather_fusion
  90.7 1.8 select_add_fusion.2
  93.7 2.3 gather_fusion
  96.0 1.8 select_add_fusion.2
  99.0 2.3 gather_fusion
  101.3 1.8 select_add_fusion.2
  104.3 2.3 gather_fusion
  109.6 2.3 gather_fusion
  111.9 1.8 select_add_fusion.2
  114.9 2.3 gather_fusion
  117.2 1.8 select_add_fusion.2
  120.1 2.3 gather_fusion
  122.5 1.8 select_add_fusion.2
  125.4 2.3 gather_fusion
  127.8 1.8 select_add_fusion.2
  130.8 2.3 gather_fusion
  133.1 1.8 select_add_fusion.2
  136.1 2.3 gather_fusion
  138.4 1.8 select_add_fusion.2
  141.4 2.3 gather_fusion
  143.7 1.8 select_add_fusion.2
  146.7 2.3 gather_fusion
  149.0 1.8 select_add_fusion.2
  152.0 2.3 gather_fusion
  154.3 1.8 select_add_fusion.2
  157.3 2.3 gather_fusion
  159.6 1.8 select_add_fusion.2
  162.6 2.3 gather_fusion
  164.9 1.8 select_add_fusion.2
  167.9 2.3 gather_fusion
  173.2 2.3 gather_fusion
  175.5 1.8 select_add_fusion.2
  178.4 6.7 %broadcast_multiply_fusion = f32[27,256,256]{1,2,0:T(8,128)} fusion(f32[27,256,256]{1,2,0:T(8,128)} %get-tuple-element.128), kind=kLoop, calls=%fused_computation.12 | loop fusion | flops 1769472 | bytes 14155776 | tf_op jit(solution)/shard_map/mul | solution.py:68
  185.1 8.0 %copy.12 = f32[27,256,256]{2,1,0:T(8,128)} copy(f32[27,256,256]{1,2,0:T(8,128)} %broadcast_multiply_fusion) | data formatting | bytes 14155776 | tf_op jit(solution)/shard_map/mul | solution.py:68
  193.1 352.1 %fusion = f32[56,256]{1,0:T(8,128)S(1)} fusion(f32[6912,256]{1,0:T(8,128)} %bitcast.47), kind=kCustom, calls=%all-reduce-scatter | all-reduce-scatter fusion | flops 1835009 | bytes 7135232
  545.2 1.9 collective-permute-start.4
  (162 shorter events, 52.1 us)
Async XLA Ops:
  0.6 9.2 %collective-permute-start = (bf16[1,1,4,128,256]{4,3,2,1,0:T(8,128)(2,1)}, bf16[1,1,4,128,256]{4,3,2,1,0:T(8,128)(2,1)S(1)}, u32[]{:S(2)}, u32[]{:S(2)}) collective-permute-start(bf16[1,1,4,128,256]{4,3,2,1,0:T(8,128)(2,1)} %param.8), channel_id=1, source_target_pairs={{0,32},{32,64},{64,96},{1,33},{33,65},{65,97},{2,34},{34,66},{66,9... | collective-permute-start | bytes 786440 | tf_op jit(solution)/shard_map/ppermute | solution.py:17
  4.6 9.0 %collective-permute-start.1 = (bf16[1,1,4,128,256]{4,3,2,1,0:T(8,128)(2,1)}, bf16[1,1,4,128,256]{4,3,2,1,0:T(8,128)(2,1)S(1)}, u32[]{:S(2)}, u32[]{:S(2)}) collective-permute-start(bf16[1,1,4,128,256]{4,3,2,1,0:T(8,128)(2,1)} %param.8), channel_id=1, source_target_pairs={{32,0},{64,32},{96,64},{33,1},{65,33},{97,65},{34,2},{66,34},{98,6... | collective-permute-start | bytes 786440 | tf_op jit(solution)/shard_map/ppermute | solution.py:19
  13.6 13.9 %collective-permute-start.2 = (bf16[3,1,4,128,256]{4,3,2,1,0:T(8,128)(2,1)S(1)}, bf16[3,1,4,128,256]{4,3,2,1,0:T(8,128)(2,1)}, u32[]{:S(2)}, u32[]{:S(2)}) collective-permute-start(bf16[3,1,4,128,256]{4,3,2,1,0:T(8,128)(2,1)S(1)} %constant_dynamic-update-slice_fusion), channel_id=1, source_target_pairs={{0,1},{1,2},{2,3},{3,4},{4,5},{5,6},{6,7},{7,8},{8,9},{9,10},{10,1... | collective-permute-start | bytes 2359304 | tf_op jit(solution)/shard_map/ppermute | solution.py:17
  18.5 13.4 %collective-permute-start.3 = (bf16[3,1,4,128,256]{4,3,2,1,0:T(8,128)(2,1)S(1)}, bf16[3,1,4,128,256]{4,3,2,1,0:T(8,128)(2,1)}, u32[]{:S(2)}, u32[]{:S(2)}) collective-permute-start(bf16[3,1,4,128,256]{4,3,2,1,0:T(8,128)(2,1)S(1)} %constant_dynamic-update-slice_fusion), channel_id=1, source_target_pairs={{1,0},{2,1},{3,2},{4,3},{5,4},{6,5},{7,6},{8,7},{9,8},{10,9},{11,1... | collective-permute-start | bytes 2359304 | tf_op jit(solution)/shard_map/ppermute | solution.py:19
  37.7 1.8 copy-start
  43.0 1.8 copy-start
  48.3 1.8 copy-start
  53.6 1.8 copy-start
  58.9 1.8 copy-start
  64.2 1.8 copy-start
  69.5 1.8 copy-start
  74.8 1.8 copy-start
  80.1 1.8 copy-start
  85.4 1.8 copy-start
  90.7 1.8 copy-start
  96.0 1.8 copy-start
  101.3 1.8 copy-start
  106.6 1.8 copy-start
  111.9 1.8 copy-start
  117.2 1.8 copy-start
  122.5 1.8 copy-start
  127.8 1.8 copy-start
  133.1 1.8 copy-start
  138.4 1.8 copy-start
  143.7 1.8 copy-start
  149.0 1.8 copy-start
  154.3 1.8 copy-start
  159.6 1.8 copy-start
  164.9 1.8 copy-start
  170.2 1.8 copy-start
  175.5 1.8 copy-start
  545.2 8.4 %collective-permute-start.4 = (f32[56,256]{1,0:T(8,128)S(1)}, f32[56,256]{1,0:T(8,128)S(1)}, u32[]{:S(2)}, u32[]{:S(2)}) collective-permute-start(f32[56,256]{1,0:T(8,128)S(1)} %fusion), channel_id=1, source_target_pairs={{0,1},{1,2},{2,3},{3,4},{4,5},{5,6},{6,7},{7,8},{8,9},{9,10},{10,1... | collective-permute-start | bytes 172040
  547.1 6.5 %collective-permute-start.5 = (f32[56,256]{1,0:T(8,128)S(1)}, f32[56,256]{1,0:T(8,128)S(1)}, u32[]{:S(2)}, u32[]{:S(2)}) collective-permute-start(f32[56,256]{1,0:T(8,128)S(1)} %fusion), channel_id=1, source_target_pairs={{0,2},{1,3},{2,4},{3,5},{4,6},{5,7},{6,8},{7,9},{8,10},{9,11},{10,... | collective-permute-start | bytes 172040
  548.4 5.2 collective-permute-start.6
  549.7 3.9 collective-permute-start.7
  551.0 2.5 collective-permute-start.8
where the time goes:
time: 565 us; the launch traced here: 555 us
  blocking collectives  352 us (62%)
  matrix products  79.5 us (14%)
  local copies, waits for them, and re-layouts  75.1 us (13%)
  starting transfers between devices  19.2 us (3%)
  waiting for transfers between devices  14.4 us (3%)
  other arithmetic  12.3 us (2%)
    unnamed x1, blocking collectives  352 us
    gather x27, local copies, waits for them, and re-layouts, offset_step(): blocks = coarse_pool[chosen]  62 us
    dot_general x27, matrix products, offset_step(): jnp.einsum('bvo,io->bvi', blocks, matrix, preferred_element_type=jnp.floa...  47.5 us
    dot_general x27, matrix products, offset_step(): jnp.einsum('bvi,bvo->io', fine_rows, blocks, preferred_element_type=jnp.f...  31.9 us
  transfers between devices with their start and end apart: 9, of which 4 were waited for; matrix products, arithmetic and copies ran while one was open for 1% of the time, Pallas kernels for 0%

commit v1 on v0

v1 whole, which is shorter than its diff:
```python
import functools
import math

import jax
import jax.numpy as jnp
from jax import lax
from jax.experimental import pallas as pl
from jax.experimental.pallas import tpu as pltpu
from jax.sharding import PartitionSpec as P

MESH = pl.DeviceIdType.MESH
F32, BF16, I16 = jnp.float32, jnp.bfloat16, jnp.int16
K, C, BLOCK, SLOTS, COARSE = 27, 256, 128, 16, 4
HALF = C // 2
GROUPS, PER_GROUP = 3, 9
PIECES, PIECE = 16, 432
LONG = PIECE + 16
YROWS = 128
YLONG = YROWS + 16
MINE = 54
LEVELS = 32767.0

dot = functools.partial(jnp.dot, preferred_element_type=F32)


def encode(values):
    top = jnp.maximum(jnp.max(jnp.abs(values), axis=0, keepdims=True), 1e-35)
    power = jnp.ceil(jnp.log2(top) + 1e-3)
    codes = jnp.floor(values * (jnp.exp2(-power) * LEVELS) + 0.5).astype(jnp.int32)
    return codes.astype(I16), jnp.broadcast_to(power, (16, HALF)).astype(jnp.int32).astype(I16)


def decode(ref, rows):
    power = ref[rows : rows + 16, :].astype(jnp.int32).astype(F32)[0:1, :]
    return ref[0:rows, :].astype(jnp.int32).astype(F32) * (jnp.exp2(power) * (1.0 / LEVELS))


def kernel(
    fine_hbm, coarse_hbm, map_ref, counts_ref, weight_hbm,
    fine_out, weight_out,
    pool, fine_in, fine_t, weight_in, weight_t, acc, from_mate,
    send1, recv1, total1, send2, recv2, total2, send3, recv3, total3,
    own_rows, mate_rows, fine_vmem, weight_vmem,
    load_sem, hx_send, hx_recv, hy_send, hy_recv, m_send, m_recv,
    s1_send, s1_recv, s2_send, s2_recv, s3_send, s3_recv, f_sem,
    out_sem,
):
    gx, gy = lax.axis_index("gx"), lax.axis_index("gy")
    z, y, c = gy // 8, (gy // 2) % 4, gy % 2

    def at(x_, z_, y_, c_):
        return (x_, z_ * 8 + y_ * 2 + c_)

    mate = at(gx, z, y, 1 - c)
    up, down = (gx, (gy + 1) % 32), (gx, (gy + 31) % 32)
    away = (gx, (gy + jnp.where(c == 0, 31, 1)) % 32)

    loads = [
        pltpu.make_async_copy(coarse_hbm, pool.at[16:20], load_sem.at[0]),
        pltpu.make_async_copy(fine_hbm, fine_in, load_sem.at[1]),
        pltpu.make_async_copy(weight_hbm, weight_in, load_sem.at[2]),
    ]
    for copy in loads:
        copy.start()

    barrier = pltpu.get_barrier_semaphore()
    partners = [mate, away]
    for d in (1, 2, 3):
        partners += [at((gx + d) % 4, z, y, c), at(gx, (z + d) % 4, y, c), at(gx, z, (y + d) % 4, c)]
    for who in partners:
        pl.semaphore_signal(barrier, inc=1, device_id=who, device_id_type=MESH)
    pl.semaphore_wait(barrier, len(partners))

    def remote(src, dst, send, recv, who):
        return pltpu.make_async_remote_copy(
            src_ref=src, dst_ref=dst, send_sem=send, recv_sem=recv, device_id=who, device_id_type=MESH
        )

    def region(r):
        return pool.at[4 * r : 4 * r + 4]

    halo = []
    for i, (who, r) in enumerate(((((gx + 1) % 4, gy), 1), (((gx + 3) % 4, gy), 7))):
        copy = remote(coarse_hbm, region(r), hx_send.at[i], hx_recv.at[i], who)
        copy.start()
        halo.append(copy)

    def along_y(p, src):
        for i, (who, q) in enumerate(((up, 0), (down, 2))):
            copy = remote(src, region(3 * p + q), hy_send.at[i, p], hy_recv.at[i, p], who)
            copy.start()
            halo_y.append(copy)

    halo_y = []
    along_y(1, coarse_hbm)

    pool[36] = jnp.zeros((BLOCK, C), BF16)
    count = counts_ref[0, 0]
    loads[1].wait()
    for f in range(SLOTS):
        block = jnp.where(f < count, fine_in[f], jnp.zeros((), BF16))
        fine_t[:, f * BLOCK : (f + 1) * BLOCK] = block.T

    halo[0].wait_recv()
    along_y(0, region(1))
    halo[1].wait_recv()
    along_y(2, region(7))
    loads[2].wait()

    def turn(k, carry):
        weight_t[pl.ds(pl.multiple_of(k * C, C), C), :] = weight_in[k].T
        return carry

    lax.fori_loop(0, K, turn, 0)
    loads[0].wait()
    for copy in halo:
        copy.wait_send()
    for copy in halo_y:
        copy.wait()

    @pl.when(gx == 0)
    def _():
        pool[0:12] = jnp.zeros((12, BLOCK, C), BF16)

    @pl.when(gx == 3)
    def _():
        pool[24:36] = jnp.zeros((12, BLOCK, C), BF16)

    for edge, q in ((0, 0), (31, 2)):

        @pl.when(gy == edge)
        def _():
            for p in range(3):
                r = 3 * p + q
                pool[4 * r : 4 * r + 4] = jnp.zeros((4, BLOCK, C), BF16)

    def chosen(k, f):
        return jnp.clip(map_ref[k, f], 0, 36)

    def weight_group(g):
        for j in range(PER_GROUP):
            k = g * PER_GROUP + j
            total = None
            for s in range(SLOTS // 2):
                pair = jnp.concatenate([pool[chosen(k, 2 * s)], pool[chosen(k, 2 * s + 1)]], axis=0)
                part = dot(fine_t[:, s * C : (s + 1) * C], pair)
                total = part if total is None else total + part
            total = total * (1.0 / math.sqrt(262144))
            acc[0, pl.ds(pl.multiple_of(k * C, C), C), :] = total[:, :HALF]
            acc[1, pl.ds(pl.multiple_of(k * C, C), C), :] = total[:, HALF:]

    def mate_copy(g):
        rows = pl.ds(pl.multiple_of(g * PER_GROUP * C, PER_GROUP * C), PER_GROUP * C)
        return remote(acc.at[1 - c, rows], from_mate.at[rows], m_send.at[g], m_recv.at[g], mate)

    first_at = jnp.where(c == 0, gx, z)
    second_at = jnp.where(c == 0, z, gx)

    def first_peer(a):
        return at(jnp.where(c == 0, a, gx), jnp.where(c == 0, z, a), y, c)

    def second_peer(b):
        return at(jnp.where(c == 0, gx, b), jnp.where(c == 0, b, z), y, c)

    def first_copy(a, b):
        slot = (first_at - a + 4) % 4 - 1
        return remote(send1.at[a, b], recv1.at[slot, b], s1_send.at[a, b], s1_recv.at[slot, b], first_peer(a))

    def ab(n):
        return jnp.where(c == 0, n // 4, n % 4), jnp.where(c == 0, n % 4, n // 4)

    def send_piece(n, carry):
        a, b = ab(n)
        rows = pl.ds(pl.multiple_of(n * PIECE, 16), PIECE)
        summed = acc[c, rows, :] + from_mate[rows, :]

        @pl.when(a == first_at)
        def _():
            total1[b] = summed

        @pl.when(a != first_at)
        def _():
            codes, scale = encode(summed)
            send1[a, b, 0:PIECE, :] = codes
            send1[a, b, PIECE:LONG, :] = scale
            first_copy(a, b).start()

        return carry

    def weight_step(g, carry):
        weight_group(g)
        mate_copy(g).start()
        return carry

    bounds = (0, 5, 10, 16)

    def send_group(g):
        mate_copy(g).wait_recv()
        lax.fori_loop(bounds[g], bounds[g + 1], send_piece, 0)

    weight_step(0, 0)
    weight_step(1, 0)
    send_group(0)
    weight_step(2, 0)
    send_group(1)
    send_group(2)

    def fine_part(s, width):
        rows = []
        for f in range(width):
            rows.append(jnp.concatenate([pool[chosen(k, s * width + f)] for k in range(K)], axis=1))
        got = dot(jnp.concatenate(rows, axis=0), weight_t[...]).astype(BF16)
        for f in range(width):
            slot = s * width + f
            fine_vmem[slot] = jnp.where(
                slot < count, got[f * BLOCK : (f + 1) * BLOCK], jnp.zeros((), BF16)
            )

    def fine_copy(s, width):
        return pltpu.make_async_copy(
            fine_vmem.at[pl.ds(s * width, width)], fine_out.at[pl.ds(s * width, width)], out_sem.at[s]
        )

    fine_part(0, 8)
    fine_copy(0, 8).start()

    def second_copy(b):
        slot = (second_at - b + 4) % 4 - 1
        return remote(send2.at[b], recv2.at[slot], s2_send.at[b], s2_recv.at[slot], second_peer(b))

    def second_step(b, carry):
        for slot in range(3):
            remote(recv1.at[slot, b], recv1.at[slot, b], s1_send.at[0, 0], s1_recv.at[slot, b], mate).wait_recv()
        summed = total1[b]
        for slot in range(3):
            summed = summed + decode(recv1.at[slot, b], PIECE)

        @pl.when(b == second_at)
        def _():
            total2[...] = summed

        @pl.when(b != second_at)
        def _():
            codes, scale = encode(summed)
            send2[b, 0:PIECE, :] = codes
            send2[b, PIECE:LONG, :] = scale
            second_copy(b).start()

        return carry

    lax.fori_loop(0, 4, second_step, 0)

    fine_part(1, 8)
    fine_copy(1, 8).start()

    starts = (0, 96, 208, 304)
    start = jnp.where(y == 0, 0, jnp.where(y == 1, 96, jnp.where(y == 2, 208, 304)))
    offset = y * 108 - start
    for slot in range(3):
        remote(recv2.at[slot], recv2.at[slot], s2_send.at[0], s2_recv.at[slot], mate).wait_recv()
    summed = total2[...]
    for slot in range(3):
        summed = summed + decode(recv2.at[slot], PIECE)
    total2[...] = summed

    def third_copy(t):
        slot = (y - t + 4) % 4 - 1
        return remote(send3.at[t], recv3.at[slot], s3_send.at[t], s3_recv.at[slot], at(gx, z, t, c))

    for t in range(4):

        @pl.when(y != t)
        def _():
            codes, scale = encode(total2[starts[t] : starts[t] + YROWS, :])
            send3[t, 0:YROWS, :] = codes
            send3[t, YROWS:YLONG, :] = scale
            third_copy(t).start()

    summed = total2[pl.ds(pl.multiple_of(start, 16), YROWS), :]
    for slot in range(3):
        remote(recv3.at[slot], recv3.at[slot], s3_send.at[0], s3_recv.at[slot], mate).wait_recv()
        summed = summed + decode(recv3.at[slot], YROWS)
    total3[...] = summed

    own_rows[0:MINE, :] = total3[pl.ds(offset + MINE * (1 - c), MINE), :]
    last = remote(own_rows, mate_rows, f_sem.at[0], f_sem.at[1], mate)
    last.start()
    weight_vmem[:, pl.ds(pl.multiple_of(c * HALF, HALF), HALF)] = total3[pl.ds(offset + MINE * c, MINE), :]
    last.wait_recv()
    weight_vmem[:, pl.ds(pl.multiple_of((1 - c) * HALF, HALF), HALF)] = mate_rows[0:MINE, :]
    final = pltpu.make_async_copy(weight_vmem, weight_out, out_sem.at[2])
    final.start()

    for g in range(GROUPS):
        mate_copy(g).wait_send()

    def drain(n, carry):
        a, b = ab(n)

        @pl.when(a != first_at)
        def _():
            first_copy(a, b).wait_send()

        return carry

    lax.fori_loop(0, PIECES, drain, 0)
    for t in range(4):

        @pl.when(second_at != t)
        def _():
            second_copy(t).wait_send()

        @pl.when(y != t)
        def _():
            third_copy(t).wait_send()

    last.wait_send()
    fine_copy(0, 8).wait()
    fine_copy(1, 8).wait()
    final.wait()


def local(fine_feat, coarse_grad, kernel_map, counts, weight):
    anywhere = pl.BlockSpec(memory_space=pl.ANY)
    smem = pl.BlockSpec(memory_space=pltpu.SMEM)
    dma = pltpu.SemaphoreType.DMA
    fine, weight_grad = pl.pallas_call(
        kernel,
        out_shape=(
            jax.ShapeDtypeStruct((SLOTS, BLOCK, C), BF16),
            jax.ShapeDtypeStruct((MINE, C), F32),
        ),
        in_specs=[anywhere, anywhere, smem, smem, anywhere],
        out_specs=(anywhere, anywhere),
        scratch_shapes=[
            pltpu.VMEM((37, BLOCK, C), BF16),
            pltpu.VMEM((SLOTS, BLOCK, C), BF16),
            pltpu.VMEM((C, SLOTS * BLOCK), BF16),
            pltpu.VMEM((K, C, C), BF16),
            pltpu.VMEM((K * C, C), BF16),
            pltpu.VMEM((2, K * C, HALF), F32),
            pltpu.VMEM((K * C, HALF), F32),
            pltpu.VMEM((4, 4, LONG, HALF), I16),
            pltpu.VMEM((3, 4, LONG, HALF), I16),
            pltpu.VMEM((4, PIECE, HALF), F32),
            pltpu.VMEM((4, LONG, HALF), I16),
            pltpu.VMEM((3, LONG, HALF), I16),
            pltpu.VMEM((PIECE, HALF), F32),
            pltpu.VMEM((4, YLONG, HALF), I16),
            pltpu.VMEM((3, YLONG, HALF), I16),
            pltpu.VMEM((YROWS, HALF), F32),
            pltpu.VMEM((56, HALF), F32),
            pltpu.VMEM((56, HALF), F32),
            pltpu.VMEM((SLOTS, BLOCK, C), BF16),
            pltpu.VMEM((MINE, C), F32),
            dma((3,)), dma((2,)), dma((2,)), dma((2, 3)), dma((2, 3)), dma((GROUPS,)), dma((GROUPS,)),
            dma((4, 4)), dma((3, 4)), dma((4,)), dma((3,)), dma((4,)), dma((3,)), dma((2,)),
            dma((3,)),
        ],
        compiler_params=pltpu.CompilerParams(
            collective_id=0, has_side_effects=True, vmem_limit_bytes=56 << 20
        ),
        cost_estimate=pl.CostEstimate(flops=14_500_000_000, bytes_accessed=8_000_000, transcendentals=0),
    )(fine_feat[0, 0], coarse_grad[0, 0], kernel_map[0, 0], counts, weight)
    return fine[None, None], weight_grad


def solution(mesh):
    return jax.shard_map(
        local,
        mesh=mesh,
        in_specs=(
            P("gx", "gy", None, None, None),
            P("gx", "gy", None, None, None),
            P("gx", "gy", None, None),
            P("gx", "gy"),
            P(),
        ),
        out_specs=(P("gx", "gy", None, None, None), P(("gx", "gy"), None)),
        check_vma=False,
    )
```

time: 565 us -> 69.3 us (0.12)
  the two profiles are of different devices: /device:TPU:1 before, /device:TPU:7 now
where the time goes in v1:
time: 69.3 us; the launch traced here: 69 us
  Pallas kernels  62.6 us (90%)
  local copies, waits for them, and re-layouts  5.11 us (7%)
  between operations  1.29 us (2%)
    pallas_call x1, Pallas kernels, local(): pl.pallas_call(kernel, out_shape=(jax.ShapeDtypeStruct((SLOTS, BLOCK, C),...  62.6 us
    unnamed x3, local copies, waits for them, and re-layouts  5.11 us

profile of v1, /device:TPU:7, one launch (start us, length us, event | category | flops | bytes accessed | tf_op | source)
XLA Modules:
  0.0 69.0 jit_solution(1431202648631262333)
XLA Ops:
  1.3 1.4 %copy.7 = s32[1,1,27,16]{3,2,1,0:T(8,128)} copy(s32[1,1,27,16]{2,3,1,0:T(8,128)} %param.7) | data formatting | bytes 3456 | tf_op args[2]
  2.7 62.6 %shard_map.68 = (bf16[16,128,256]{2,1,0:T(8,128)(2,1)}, f32[54,256]{1,0:T(8,128)}) custom-call(bf16[16,128,256]{2,1,0:T(8,128)(2,1)} %bitcast.6, bf16[4,128,256]{2,1,0:T(8,128)(2,1)} %bitcast.7, s32[27,16]{1,0:T(8,128)} %bitcast.5, s32[1,1]{1,0:T(1,128)S(6)} %copy.10.counts_ref, bf16[27,256,256]{2,1,0:T(8,128)(2,1)} %weight_hbm.1), custom_call_target="tpu_custom_call" | custom-call | flops 14499999744 | bytes 8000000 | tf_op jit(solution)/shard_map/pallas_call | solution.py:327
  65.2 2.3 %copy.11 = bf16[1,1,16,128,256]{4,3,2,1,0:T(8,128)(2,1)} copy(bf16[1,1,16,128,256]{4,3,2,1,0:T(8,128)(2,1)} %bitcast.4) | data formatting | bytes 2097152
  67.5 1.4 %copy.12 = f32[54,256]{1,0:T(8,128)} copy(f32[54,256]{1,0:T(8,128)} %get-tuple-element.9) | data formatting | bytes 110592

commit v2 on v1

v2 whole, which is shorter than its diff:
```python
import functools
import math

import jax
import jax.numpy as jnp
from jax import lax
from jax.experimental import pallas as pl
from jax.experimental.pallas import tpu as pltpu
from jax.sharding import PartitionSpec as P

MESH = pl.DeviceIdType.MESH
F32, BF16, I16 = jnp.float32, jnp.bfloat16, jnp.int16
K, C, BLOCK, SLOTS, COARSE = 27, 256, 128, 16, 4
HALF = C // 2
GROUPS, PER_GROUP = 4, 7
UNIT = 108
LONG = 112
MINE = 54
LEVELS = 32767.0

dot = functools.partial(jnp.dot, preferred_element_type=F32)


def encode(values):
    held = lax.broadcasted_iota(jnp.int32, (LONG, HALF), 0) < UNIT
    top = jnp.max(jnp.where(held, jnp.abs(values), 0.0), axis=0, keepdims=True)
    power = jnp.ceil(jnp.log2(jnp.maximum(top, 1e-35)) + 1e-3)
    codes = jnp.floor(values * (jnp.exp2(-power) * LEVELS) + 0.5)
    return jnp.where(held, codes, power).astype(jnp.int32).astype(I16)


def decode(unit):
    codes = unit.astype(jnp.int32).astype(F32)
    return codes * (jnp.exp2(codes[UNIT : UNIT + 1, :]) * (1.0 / LEVELS))


def kernel(
    fine_hbm, coarse_hbm, map_ref, counts_ref, weight_hbm,
    fine_out, weight_out,
    pool, fine_in, fine_t, weight_in, weight_t, acc, from_mate,
    send1, recv1, send2, recv2, total2, total3,
    own_rows, mate_rows, fine_vmem, weight_vmem,
    load_sem, hx_send, hx_recv, hy_send, hy_recv, m_send, m_recv,
    s1_send, s1_recv, s2_send, s2_recv, f_sem, out_sem,
):
    gx, gy = lax.axis_index("gx"), lax.axis_index("gy")
    z, y, c = gy // 8, (gy // 2) % 4, gy % 2

    def at(x_, z_, y_, c_):
        return (x_, z_ * 8 + y_ * 2 + c_)

    mate = at(gx, z, y, 1 - c)
    up, down = (gx, (gy + 1) % 32), (gx, (gy + 31) % 32)
    away = (gx, (gy + jnp.where(c == 0, 31, 1)) % 32)

    loads = [
        pltpu.make_async_copy(coarse_hbm, pool.at[16:20], load_sem.at[0]),
        pltpu.make_async_copy(fine_hbm, fine_in, load_sem.at[1]),
        pltpu.make_async_copy(weight_hbm, weight_in, load_sem.at[2]),
    ]
    for copy in loads:
        copy.start()

    barrier = pltpu.get_barrier_semaphore()
    first_at = jnp.where(c == 0, z, y)
    third_at = jnp.where(c == 0, y, z)

    def first_peer(a):
        return at(gx, jnp.where(c == 0, a, z), jnp.where(c == 0, y, a), c)

    def plane_peer(b, d):
        return at(b, jnp.where(c == 0, z, d), jnp.where(c == 0, d, y), c)

    partners = [mate, away] + [first_peer((first_at + s) % 4) for s in (1, 2, 3)]
    partners += [plane_peer((gx + e // 4) % 4, (third_at + e % 4) % 4) for e in range(1, 16)]
    for who in partners:
        pl.semaphore_signal(barrier, inc=1, device_id=who, device_id_type=MESH)
    pl.semaphore_wait(barrier, len(partners))

    def remote(src, dst, send, recv, who):
        return pltpu.make_async_remote_copy(
            src_ref=src, dst_ref=dst, send_sem=send, recv_sem=recv, device_id=who, device_id_type=MESH
        )

    def region(r):
        return pool.at[4 * r : 4 * r + 4]

    halo = []

    def along_x(j):
        for i, (who, r) in enumerate(((((gx + 1) % 4, gy), 1), (((gx + 3) % 4, gy), 7))):
            copy = remote(coarse_hbm.at[j], pool.at[4 * r + j], hx_send.at[i, j], hx_recv.at[i, j], who)
            copy.start()
            halo.append((copy, i, j))

    halo_y = []

    def along_y(p, j, src):
        for i, (who, q) in enumerate(((up, 0), (down, 2))):
            at_block = 4 * (3 * p + q) + j
            copy = remote(src, pool.at[at_block], hy_send.at[i, p, j], hy_recv.at[i, p, j], who)
            copy.start()
            halo_y.append(copy)

    for j in range(COARSE):
        along_x(j)
        along_y(1, j, coarse_hbm.at[j])

    pool[36] = jnp.zeros((BLOCK, C), BF16)
    count = counts_ref[0, 0]
    loads[1].wait()
    for f in range(SLOTS):
        block = jnp.where(f < count, fine_in[f], jnp.zeros((), BF16))
        fine_t[:, f * BLOCK : (f + 1) * BLOCK] = block.T

    for copy, i, j in halo:
        copy.wait_recv()
        along_y(2 * i, j, pool.at[4 * (1 + 6 * i) + j])
    loads[2].wait()

    def turn(k, carry):
        weight_t[pl.ds(pl.multiple_of(k * C, C), C), :] = weight_in[k].T
        return carry

    lax.fori_loop(0, K, turn, 0)
    loads[0].wait()
    for copy, _, _ in halo:
        copy.wait_send()
    for copy in halo_y:
        copy.wait()

    @pl.when(gx == 0)
    def _():
        pool[0:12] = jnp.zeros((12, BLOCK, C), BF16)

    @pl.when(gx == 3)
    def _():
        pool[24:36] = jnp.zeros((12, BLOCK, C), BF16)

    for edge, q in ((0, 0), (31, 2)):

        @pl.when(gy == edge)
        def _():
            for p in range(3):
                r = 3 * p + q
                pool[4 * r : 4 * r + 4] = jnp.zeros((4, BLOCK, C), BF16)

    def chosen(k, f):
        return jnp.clip(map_ref[k, f], 0, 36)

    acc[:, K * C : K * C + 8, :] = jnp.zeros((2, 8, HALF), F32)
    from_mate[K * C : K * C + 8, :] = jnp.zeros((8, HALF), F32)

    def weight_group(g):
        for k in range(g * PER_GROUP, min(K, (g + 1) * PER_GROUP)):
            total = None
            for s in range(SLOTS // 2):
                pair = jnp.concatenate([pool[chosen(k, 2 * s)], pool[chosen(k, 2 * s + 1)]], axis=0)
                part = dot(fine_t[:, s * C : (s + 1) * C], pair)
                total = part if total is None else total + part
            total = total * (1.0 / math.sqrt(262144))
            acc[0, k * C : (k + 1) * C, :] = total[:, :HALF]
            acc[1, k * C : (k + 1) * C, :] = total[:, HALF:]
        mate_copy(g).start()

    def mate_copy(g):
        rows = pl.ds(g * PER_GROUP * C, (min(K, (g + 1) * PER_GROUP) - g * PER_GROUP) * C)
        return remote(acc.at[1 - c, rows], from_mate.at[rows], m_send.at[g], m_recv.at[g], mate)

    def summed_unit(b, a, d):
        start = UNIT * (16 * b + jnp.where(c == 0, 4 * a + d, 4 * d + a))
        return acc[c, pl.ds(start, LONG), :] + from_mate[pl.ds(start, LONG), :]

    def first_copy(a, b):
        slot = (first_at - a + 4) % 4 - 1
        return remote(send1.at[a, b], recv1.at[slot, b], s1_send.at[a, b], s1_recv.at[slot, b], first_peer(a))

    def first_stage(b):
        mate_copy(b).wait_recv()

        def step(s, carry):
            a = (first_at + s) % 4
            for d in range(4):
                send1[a, b, d] = encode(summed_unit(b, a, d))
            first_copy(a, b).start()
            return carry

        lax.fori_loop(1, 4, step, 0)

    def second_copy(b, d):
        e = 4 * ((gx - b + 4) % 4) + (third_at - d + 4) % 4 - 1
        return remote(send2.at[b, d], recv2.at[e], s2_send.at[b, d], s2_recv.at[e], plane_peer(b, d))

    def second_stage(b):
        for slot in range(3):
            remote(recv1.at[slot, b], recv1.at[slot, b], s1_send.at[0, 0], s1_recv.at[slot, b], mate).wait_recv()

        def step(d, carry):
            summed = summed_unit(b, first_at, d)
            for slot in range(3):
                summed = summed + decode(recv1[slot, b, d])
            here = (b == gx) & (d == third_at)

            @pl.when(here)
            def _():
                total2[...] = summed

            @pl.when(jnp.logical_not(here))
            def _():
                send2[b, d] = encode(summed)
                second_copy(b, d).start()

            return carry

        lax.fori_loop(0, 4, step, 0)

    def fine_part(s, width):
        rows = []
        for f in range(width):
            rows.append(jnp.concatenate([pool[chosen(k, s * width + f)] for k in range(K)], axis=1))
        got = dot(jnp.concatenate(rows, axis=0), weight_t[...]).astype(BF16)
        for f in range(width):
            slot = s * width + f
            fine_vmem[slot] = jnp.where(
                slot < count, got[f * BLOCK : (f + 1) * BLOCK], jnp.zeros((), BF16)
            )

    def fine_copy(s, width):
        return pltpu.make_async_copy(
            fine_vmem.at[pl.ds(s * width, width)], fine_out.at[pl.ds(s * width, width)], out_sem.at[s]
        )

    def fine_step(s):
        fine_part(s, 4)
        fine_copy(s, 4).start()


    weight_group(0)
    weight_group(1)
    first_stage(0)
    weight_group(2)
    first_stage(1)
    weight_group(3)
    first_stage(2)
    second_stage(0)
    first_stage(3)
    second_stage(1)
    fine_step(0)
    second_stage(2)
    fine_step(1)
    second_stage(3)
    fine_step(2)
    fine_step(3)

    def last_step(e, summed):
        remote(recv2.at[e], recv2.at[e], s2_send.at[0, 0], s2_recv.at[e], mate).wait_recv()
        return summed + decode(recv2[e])

    total3[...] = lax.fori_loop(0, 15, last_step, total2[...])

    own_rows[0:MINE, :] = total3[pl.ds(MINE * (1 - c), MINE), :]
    last = remote(own_rows, mate_rows, f_sem.at[0], f_sem.at[1], mate)
    last.start()
    weight_vmem[:, pl.ds(pl.multiple_of(c * HALF, HALF), HALF)] = total3[pl.ds(MINE * c, MINE), :]
    last.wait_recv()
    weight_vmem[:, pl.ds(pl.multiple_of((1 - c) * HALF, HALF), HALF)] = mate_rows[0:MINE, :]
    final = pltpu.make_async_copy(weight_vmem, weight_out, out_sem.at[4])
    final.start()

    for g in range(GROUPS):
        mate_copy(g).wait_send()

    def drain_first(n, carry):
        first_copy((first_at + 1 + n // 4) % 4, n % 4).wait_send()
        return carry

    lax.fori_loop(0, 12, drain_first, 0)

    def drain_second(e, carry):
        second_copy((gx + e // 4) % 4, (third_at + e % 4) % 4).wait_send()
        return carry

    lax.fori_loop(1, 16, drain_second, 0)
    last.wait_send()
    for s in range(4):
        fine_copy(s, 4).wait()
    final.wait()


def local(fine_feat, coarse_grad, kernel_map, counts, weight):
    anywhere = pl.BlockSpec(memory_space=pl.ANY)
    smem = pl.BlockSpec(memory_space=pltpu.SMEM)
    dma = pltpu.SemaphoreType.DMA
    fine, weight_grad = pl.pallas_call(
        kernel,
        out_shape=(
            jax.ShapeDtypeStruct((SLOTS, BLOCK, C), BF16),
            jax.ShapeDtypeStruct((MINE, C), F32),
        ),
        in_specs=[anywhere, anywhere, smem, smem, anywhere],
        out_specs=(anywhere, anywhere),
        scratch_shapes=[
            pltpu.VMEM((37, BLOCK, C), BF16),
            pltpu.VMEM((SLOTS, BLOCK, C), BF16),
            pltpu.VMEM((C, SLOTS * BLOCK), BF16),
            pltpu.VMEM((K, C, C), BF16),
            pltpu.VMEM((K * C, C), BF16),
            pltpu.VMEM((2, K * C + 8, HALF), F32),
            pltpu.VMEM((K * C + 8, HALF), F32),
            pltpu.VMEM((4, 4, 4, LONG, HALF), I16),
            pltpu.VMEM((3, 4, 4, LONG, HALF), I16),
            pltpu.VMEM((4, 4, LONG, HALF), I16),
            pltpu.VMEM((15, LONG, HALF), I16),
            pltpu.VMEM((LONG, HALF), F32),
            pltpu.VMEM((LONG, HALF), F32),
            pltpu.VMEM((56, HALF), F32),
            pltpu.VMEM((56, HALF), F32),
            pltpu.VMEM((SLOTS, BLOCK, C), BF16),
            pltpu.VMEM((MINE, C), F32),
            dma((3,)), dma((2, 4)), dma((2, 4)), dma((2, 3, 4)), dma((2, 3, 4)), dma((GROUPS,)), dma((GROUPS,)),
            dma((4, 4)), dma((3, 4)), dma((4, 4)), dma((15,)), dma((2,)), dma((5,)),
        ],
        compiler_params=pltpu.CompilerParams(
            collective_id=0, has_side_effects=True, vmem_limit_bytes=56 << 20
        ),
        cost_estimate=pl.CostEstimate(flops=14_500_000_000, bytes_accessed=8_000_000, transcendentals=0),
    )(fine_feat[0, 0], coarse_grad[0, 0], kernel_map[0, 0], counts, weight)
    return fine[None, None], weight_grad


def solution(mesh):
    return jax.shard_map(
        local,
        mesh=mesh,
        in_specs=(
            P("gx", "gy", None, None, None),
            P("gx", "gy", None, None, None),
            P("gx", "gy", None, None),
            P("gx", "gy"),
            P(),
        ),
        out_specs=(P("gx", "gy", None, None, None), P(("gx", "gy"), None)),
        check_vma=False,
    )
```

time: 69.3 us -> 59 us (0.85)
  the two profiles are of different devices: /device:TPU:7 before, /device:TPU:1 now
where the time goes in v2:
time: 59 us; the launch traced here: 57.9 us
  Pallas kernels  51.5 us (87%)
  local copies, waits for them, and re-layouts  5.11 us (9%)
  between operations  1.29 us (2%)
    pallas_call x1, Pallas kernels, local(): pl.pallas_call(kernel, out_shape=(jax.ShapeDtypeStruct((SLOTS, BLOCK, C),...  51.5 us
    unnamed x3, local copies, waits for them, and re-layouts  5.11 us

profile of v2, /device:TPU:1, one launch (start us, length us, event | category | flops | bytes accessed | tf_op | source)
XLA Modules:
  0.0 57.9 jit_solution(17755505166743797277)
XLA Ops:
  1.3 1.4 %copy.7 = s32[1,1,27,16]{3,2,1,0:T(8,128)} copy(s32[1,1,27,16]{2,3,1,0:T(8,128)} %param.7) | data formatting | bytes 3456 | tf_op args[2]
  2.7 51.5 %shard_map.68 = (bf16[16,128,256]{2,1,0:T(8,128)(2,1)}, f32[54,256]{1,0:T(8,128)}) custom-call(bf16[16,128,256]{2,1,0:T(8,128)(2,1)} %bitcast.6, bf16[4,128,256]{2,1,0:T(8,128)(2,1)} %bitcast.7, s32[27,16]{1,0:T(8,128)} %bitcast.5, s32[1,1]{1,0:T(1,128)S(6)} %copy.10.counts_ref, bf16[27,256,256]{2,1,0:T(8,128)(2,1)} %weight_hbm.1), custom_call_target="tpu_custom_call" | custom-call | flops 14499999744 | bytes 8000000 | tf_op jit(solution)/shard_map/pallas_call | solution.py:294
  54.2 2.3 %copy.11 = bf16[1,1,16,128,256]{4,3,2,1,0:T(8,128)(2,1)} copy(bf16[1,1,16,128,256]{4,3,2,1,0:T(8,128)(2,1)} %bitcast.4) | data formatting | bytes 2097152
  56.4 1.4 %copy.12 = f32[54,256]{1,0:T(8,128)} copy(f32[54,256]{1,0:T(8,128)} %get-tuple-element.9) | data formatting | bytes 110592

commit v3 on v2

v3 whole, which is shorter than its diff:
```python
import functools
import math

import jax
import jax.numpy as jnp
from jax import lax
from jax.experimental import pallas as pl
from jax.experimental.pallas import tpu as pltpu
from jax.sharding import PartitionSpec as P

MESH = pl.DeviceIdType.MESH
F32, BF16, I16 = jnp.float32, jnp.bfloat16, jnp.int16
K, C, BLOCK, SLOTS, COARSE = 27, 256, 128, 16, 4
HALF = C // 2
ENDS = (8, 15, 21, 27)
UNIT = 108
LONG = 112
MINE = 54
ROWS = 64
LEVELS = 32767.0

dot = functools.partial(jnp.dot, preferred_element_type=F32)


def encode(values):
    held = lax.broadcasted_iota(jnp.int32, (LONG, HALF), 0) < UNIT
    top = jnp.max(jnp.where(held, jnp.abs(values), 0.0), axis=0, keepdims=True)
    power = jnp.ceil(jnp.log2(jnp.maximum(top, 1e-35)) + 1e-3)
    codes = jnp.floor(values * (jnp.exp2(-power) * LEVELS) + 0.5)
    return jnp.where(held, codes, power).astype(jnp.int32).astype(I16)


def decode(unit):
    codes = unit.astype(jnp.int32).astype(F32)
    return codes * (jnp.exp2(codes[UNIT : UNIT + 1, :]) * (1.0 / LEVELS))


def kernel(
    fine_hbm, coarse_hbm, map_ref, counts_ref, weight_hbm,
    fine_out, weight_out,
    pool_low, pool_high, fine_in, fine_t, weight_in, weight_t, acc, from_mate,
    send1, recv1, send2, recv2, send3, recv3, total2, total3,
    own_rows, mate_rows,
    load_sem, hx_send, hx_recv, hy_send, hy_recv, m_send, m_recv,
    s1_send, s1_recv, s2_send, s2_recv, s3_send, s3_recv, f_sem,
):
    pools = (pool_low, pool_high)
    gx, gy = lax.axis_index("gx"), lax.axis_index("gy")
    z, y, c = gy // 8, (gy // 2) % 4, gy % 2

    def at(x_, z_, y_, c_):
        return (x_, z_ * 8 + y_ * 2 + c_)

    mate = at(gx, z, y, 1 - c)
    up, down = (gx, (gy + 1) % 32), (gx, (gy + 31) % 32)
    away = (gx, (gy + jnp.where(c == 0, 31, 1)) % 32)

    loads = [
        pltpu.make_async_copy(coarse_hbm.at[:, 0:ROWS], pool_low.at[16:20], load_sem.at[0]),
        pltpu.make_async_copy(fine_hbm, fine_in, load_sem.at[1]),
        pltpu.make_async_copy(weight_hbm, weight_in, load_sem.at[2]),
        pltpu.make_async_copy(coarse_hbm.at[:, ROWS:BLOCK], pool_high.at[16:20], load_sem.at[3]),
    ]
    for copy in loads:
        copy.start()

    barrier = pltpu.get_barrier_semaphore()
    first_at = jnp.where(c == 0, z, y)
    third_at = jnp.where(c == 0, y, z)

    def first_peer(a):
        return at(gx, jnp.where(c == 0, a, z), jnp.where(c == 0, y, a), c)

    def third_peer(d):
        return at(gx, jnp.where(c == 0, z, d), jnp.where(c == 0, d, y), c)

    partners = [mate, away]
    for s in (1, 2, 3):
        partners += [first_peer((first_at + s) % 4), ((gx + s) % 4, gy), third_peer((third_at + s) % 4)]
    for who in partners:
        pl.semaphore_signal(barrier, inc=1, device_id=who, device_id_type=MESH)
    pl.semaphore_wait(barrier, len(partners))

    def remote(src, dst, send, recv, who):
        return pltpu.make_async_remote_copy(
            src_ref=src, dst_ref=dst, send_sem=send, recv_sem=recv, device_id=who, device_id_type=MESH
        )

    ORDER = [(h, j) for h in range(2) for j in range(2)]

    def own(h, j):
        return coarse_hbm.at[pl.ds(2 * j, 2), pl.ds(ROWS * h, ROWS)]

    def part(r, h, j):
        return pools[h].at[pl.ds(4 * r + 2 * j, 2)]

    def x_copy(i, h, j):
        who, r = (((gx + 1) % 4, gy), 1) if i == 0 else (((gx + 3) % 4, gy), 7)
        return remote(own(h, j), part(r, h, j), hx_send.at[i, h, j], hx_recv.at[i, h, j], who)

    def y_copy(i, p, h, j):
        who = (gx, (gy + jnp.where(i == 0, 1, 31)) % 32)
        src = own(h, j) if p == 1 else part(3 * p + 1, h, j)
        return remote(src, part(3 * p + 2 * i, h, j), hy_send.at[i, p, h, j], hy_recv.at[i, p, h, j], who)

    def corner_copy(p):
        who = ((gx + 1 + p) % 4, gy)
        src, dst = part(3 + 2 * c, 1, 1), part(3 * p + 2 * c, 1, 1)
        return remote(src, dst, hy_send.at[1 - c, p, 1, 1], hy_recv.at[c, p, 1, 1], who)

    def own_along_y(h, j):
        for i in range(2):
            y_copy(i, 1, h, j).start()

    for h, j in ORDER:
        for i in range(2):
            x_copy(i, h, j).start()
    own_along_y(0, 0)
    own_along_y(0, 1)
    own_along_y(1, 1)

    def forward(h, j):
        for p in (0, 2):
            x_copy(p // 2, h, j).wait_recv()
            if (h, j) == (1, 1):
                y_copy(c, p, h, j).start()
            else:
                for i in range(2):
                    y_copy(i, p, h, j).start()

    def halo_done(h):
        for j in range(2):
            for i in range(2):
                for p in range(3):
                    if (p, h, j) != (1, 1, 1):
                        y_copy(i, p, h, j).wait_recv()
                for p in (0, 2):
                    y_copy(i, p, h, j).wait_send()

        @pl.when(gx == 0)
        def _():
            pools[h][0:12] = jnp.zeros((12, ROWS, C), BF16)

        @pl.when(gx == 3)
        def _():
            pools[h][24:36] = jnp.zeros((12, ROWS, C), BF16)

        for edge, q in ((0, 0), (31, 2)):

            @pl.when(gy == edge)
            def _():
                for p in range(3):
                    r = 3 * p + q
                    pools[h][4 * r : 4 * r + 4] = jnp.zeros((4, ROWS, C), BF16)

    for pool in pools:
        pool[36] = jnp.zeros((ROWS, C), BF16)
    count = counts_ref[0, 0]
    loads[1].wait()
    for f in range(SLOTS // 4):
        blocks = [jnp.where(4 * f + i < count, fine_in[4 * f + i], jnp.zeros((), BF16)) for i in range(4)]
        for h in range(2):
            quad = jnp.concatenate([block[ROWS * h : ROWS * (h + 1)] for block in blocks], axis=0)
            fine_t[h, :, f * C : (f + 1) * C] = quad.T
    acc[:, K * C : K * C + 8, :] = jnp.zeros((2, 8, HALF), F32)
    from_mate[K * C : K * C + 8, :] = jnp.zeros((8, HALF), F32)
    loads[0].wait()
    loads[3].wait()
    loads[2].wait()

    def turn(k, carry):
        weight_t[pl.ds(pl.multiple_of(k * C, C), C), :] = weight_in[k].T
        return carry

    forward(0, 0)
    lax.fori_loop(0, 9, turn, 0)
    forward(0, 1)
    own_along_y(1, 0)
    for i in range(2):
        y_copy(i, 1, 1, 1).wait_recv()
    for p in (0, 2):
        corner_copy(p).start()
    lax.fori_loop(9, 18, turn, 0)
    forward(1, 0)
    lax.fori_loop(18, K, turn, 0)
    forward(1, 1)
    halo_done(0)

    def chosen(k, f):
        return jnp.clip(map_ref[f, k], 0, 36)

    def weight_offset(k, h):
        total = None
        for s in range(SLOTS // 4):
            quad = [pools[h][chosen(k, 4 * s + i)] for i in range(4)]
            piece = dot(fine_t[h, :, s * C : (s + 1) * C], jnp.concatenate(quad, axis=0))
            total = piece if total is None else total + piece
        return total * (1.0 / math.sqrt(262144))

    def first_half(g, carry):
        for i in range(9):
            k = 9 * g + i
            total = weight_offset(k, 0)
            for side in range(2):
                acc[side, pl.ds(pl.multiple_of(k * C, C), C), :] = total[:, side * HALF : (side + 1) * HALF]
        return carry

    begin = (gx + 1) % 4
    begin = jnp.where(begin == 0, 0, jnp.where(begin == 1, 6, jnp.where(begin == 2, 13, 20)))

    def rows_of(n):
        return pl.ds(pl.multiple_of((begin + n) % K * C, C), C)

    def mate_copy(n):
        rows = rows_of(n)
        return remote(acc.at[1 - c, rows], from_mate.at[rows], m_send.at[n], m_recv.at[n], mate)

    def members(g):
        return range(0 if g == 0 else ENDS[g - 1], ENDS[g])

    def weight_group(start, end):
        for n in range(start, end):
            total = weight_offset((begin + n) % K, 1)
            for side in range(2):
                acc[side, rows_of(n), :] += total[:, side * HALF : (side + 1) * HALF]
        for n in range(start, end):
            mate_copy(n).start()

    def summed_unit(g, a, d):
        start = UNIT * (16 * ((gx + 1 + g) % 4) + jnp.where(c == 0, 4 * a + d, 4 * d + a))
        return acc[c, pl.ds(start, LONG), :] + from_mate[pl.ds(start, LONG), :]

    def first_copy(g, s):
        who = first_peer((first_at + s) % 4)
        return remote(send1.at[s - 1, g], recv1.at[3 - s, g], s1_send.at[s - 1, g], s1_recv.at[3 - s, g], who)

    def first_stage(g):
        for n in members(g):
            mate_copy(n).wait_recv()
        for s in (2, 1, 3):
            for d in range(4):
                send1[s - 1, g, d] = encode(summed_unit(g, (first_at + s) % 4, d))
            first_copy(g, s).start()

    def second_copy(g):
        return remote(send2.at[g], recv2.at[g], s2_send.at[g], s2_recv.at[g], ((gx + 1 + g) % 4, gy))

    def third_copy(d):
        slot = (third_at - d + 4) % 4 - 1
        return remote(send3.at[d], recv3.at[slot], s3_send.at[d], s3_recv.at[slot], third_peer(d))

    def second_stage(g):
        for s in (1, 2, 3):
            first_copy(g, s).wait_recv()
        if g == 3:
            for slot in range(3):
                second_copy(slot).wait_recv()
        for d in range(4):
            summed = summed_unit(g, first_at, d)
            for slot in range(3):
                summed = summed + decode(recv1[slot, g, d])
            if g < 3:
                send2[g, d] = encode(summed)
                continue
            for slot in range(3):
                summed = summed + decode(recv2[slot, d])

            @pl.when(d == third_at)
            def _():
                total2[...] = summed

            @pl.when(d != third_at)
            def _():
                send3[d] = encode(summed)
                third_copy(d).start()

        if g < 3:
            second_copy(g).start()

    def fine_part(s, width):
        rows = []
        for f in range(width):
            for pool in pools:
                rows.append(jnp.concatenate([pool[chosen(k, s * width + f)] for k in range(K)], axis=1))
        got = dot(jnp.concatenate(rows, axis=0), weight_t[...]).astype(BF16)
        for f in range(width):
            slot = s * width + f
            fine_out[slot] = jnp.where(
                slot < count, got[f * BLOCK : (f + 1) * BLOCK], jnp.zeros((), BF16)
            )

    def fine_step(s):
        fine_part(s, 2)


    lax.fori_loop(0, 3, first_half, 0)
    halo_done(1)
    weight_group(0, 4)
    weight_group(4, 8)
    weight_group(8, 15)
    first_stage(0)
    weight_group(15, 21)
    first_stage(1)
    weight_group(21, 27)
    first_stage(2)
    fine_step(0)
    first_stage(3)
    second_stage(0)
    fine_step(1)
    fine_step(2)
    second_stage(1)
    fine_step(3)
    fine_step(4)
    second_stage(2)
    fine_step(5)
    fine_step(6)
    second_stage(3)
    fine_step(7)

    summed = total2[...]
    for e in range(3):
        remote(recv3.at[e], recv3.at[e], s3_send.at[0], s3_recv.at[e], mate).wait_recv()
        summed = summed + decode(recv3[e])
    total3[...] = summed

    own_rows[0:MINE, :] = total3[pl.ds(MINE * (1 - c), MINE), :]
    last = remote(own_rows, mate_rows, f_sem.at[0], f_sem.at[1], mate)
    last.start()
    weight_out[:, pl.ds(pl.multiple_of(c * HALF, HALF), HALF)] = total3[pl.ds(MINE * c, MINE), :]
    last.wait_recv()
    weight_out[:, pl.ds(pl.multiple_of((1 - c) * HALF, HALF), HALF)] = mate_rows[0:MINE, :]

    for h, j in ORDER:
        for i in range(2):
            x_copy(i, h, j).wait_send()
            y_copy(i, 1, h, j).wait_send()

    def drain_mate(n, carry):
        mate_copy(n).wait_send()
        return carry

    lax.fori_loop(0, K, drain_mate, 0)
    for g in range(4):
        for s in (1, 2, 3):
            first_copy(g, s).wait_send()
        if g < 3:
            second_copy(g).wait_send()

        @pl.when(g != third_at)
        def _():
            third_copy(g).wait_send()

    last.wait_send()


def finish(fine_in, weight_in, fine_out, weight_out, sems):
    copies = [pltpu.make_async_copy(weight_in, weight_out, sems.at[4])]
    for s in range(4):
        rows = pl.ds(4 * s, 4)
        copies.append(pltpu.make_async_copy(fine_in.at[rows], fine_out.at[rows], sems.at[s]))
    for copy in copies:
        copy.start()
    for copy in copies:
        copy.wait()


def local(fine_feat, coarse_grad, kernel_map, counts, weight):
    anywhere = pl.BlockSpec(memory_space=pl.ANY)
    smem = pl.BlockSpec(memory_space=pltpu.SMEM)
    vmem = pl.BlockSpec(memory_space=pltpu.VMEM)
    dma = pltpu.SemaphoreType.DMA
    fine, weight_grad = pl.pallas_call(
        kernel,
        out_shape=(pltpu.VMEM((SLOTS, BLOCK, C), BF16), pltpu.VMEM((MINE, C), F32)),
        in_specs=[anywhere, anywhere, smem, smem, anywhere],
        out_specs=(vmem, vmem),
        scratch_shapes=[
            pltpu.VMEM((37, ROWS, C), BF16),
            pltpu.VMEM((37, ROWS, C), BF16),
            pltpu.VMEM((SLOTS, BLOCK, C), BF16),
            pltpu.VMEM((2, C, SLOTS * ROWS), BF16),
            pltpu.VMEM((K, C, C), BF16),
            pltpu.VMEM((K * C, C), BF16),
            pltpu.VMEM((2, K * C + 8, HALF), F32),
            pltpu.VMEM((K * C + 8, HALF), F32),
            pltpu.VMEM((3, 4, 4, LONG, HALF), I16),
            pltpu.VMEM((3, 4, 4, LONG, HALF), I16),
            pltpu.VMEM((3, 4, LONG, HALF), I16),
            pltpu.VMEM((3, 4, LONG, HALF), I16),
            pltpu.VMEM((4, LONG, HALF), I16),
            pltpu.VMEM((3, LONG, HALF), I16),
            pltpu.VMEM((LONG, HALF), F32),
            pltpu.VMEM((LONG, HALF), F32),
            pltpu.VMEM((56, HALF), F32),
            pltpu.VMEM((56, HALF), F32),
            dma((4,)), dma((2, 2, 2)), dma((2, 2, 2)), dma((2, 3, 2, 2)), dma((2, 3, 2, 2)), dma((K,)), dma((K,)),
            dma((3, 4)), dma((3, 4)), dma((3,)), dma((3,)), dma((4,)), dma((3,)), dma((2,)),
        ],
        compiler_params=pltpu.CompilerParams(
            collective_id=0, has_side_effects=True, vmem_limit_bytes=56 << 20
        ),
        cost_estimate=pl.CostEstimate(flops=14_500_000_000, bytes_accessed=8_000_000, transcendentals=0),
    )(fine_feat[0, 0], coarse_grad[0, 0], kernel_map[0, 0].T, counts, weight)
    fine, weight_grad = pl.pallas_call(
        finish,
        out_shape=(
            jax.ShapeDtypeStruct((SLOTS, BLOCK, C), BF16),
            jax.ShapeDtypeStruct((MINE, C), F32),
        ),
        in_specs=[vmem, vmem],
        out_specs=(anywhere, anywhere),
        scratch_shapes=[dma((5,))],
        compiler_params=pltpu.CompilerParams(vmem_limit_bytes=8 << 20),
    )(fine, weight_grad)
    return fine[None, None], weight_grad


def solution(mesh):
    return jax.shard_map(
        local,
        mesh=mesh,
        in_specs=(
            P("gx", "gy", None, None, None),
            P("gx", "gy", None, None, None),
            P("gx", "gy", None, None),
            P("gx", "gy"),
            P(),
        ),
        out_specs=(P("gx", "gy", None, None, None), P(("gx", "gy"), None)),
        check_vma=False,
    )
```

time: 59 us -> 49.8 us (0.84); the launches traced: 57.9 us -> 49.6 us
  local copies, waits for them, and re-layouts: 5.11 us -> 0 us
  Pallas kernels: 51.5 us -> 48.3 us
    unnamed x3 -> x0, local copies, waits for them, and re-layouts: 5.11 us -> none
    pallas_call x1 -> x2, Pallas kernels: 51.5 us -> 48.3 us  [the longest x1 47.3 us: local(): pl.pallas_call(kernel, out_shape=(pltpu.VMEM((SLOTS, BLOCK, C), BF16), pl...]
where the time goes in v3:
time: 49.8 us; the launch traced here: 49.6 us
  Pallas kernels  48.3 us (97%)
  between operations  1.28 us (3%)
    pallas_call x1, Pallas kernels, local(): pl.pallas_call(kernel, out_shape=(pltpu.VMEM((SLOTS, BLOCK, C), BF16), pl...  47.3 us
    pallas_call x1, Pallas kernels, local(): pl.pallas_call(finish, out_shape=(jax.ShapeDtypeStruct((SLOTS, BLOCK, C),...  1.02 us

profile of v3, /device:TPU:1, one launch (start us, length us, event | category | flops | bytes accessed | tf_op | source)
XLA Modules:
  0.0 49.6 jit_solution(8320651539688898599)
XLA Ops:
  1.3 47.3 %shard_map.68 = (bf16[16,128,256]{2,1,0:T(8,128)(2,1)S(1)}, f32[54,256]{1,0:T(8,128)S(1)}) custom-call(bf16[16,128,256]{2,1,0:T(8,128)(2,1)} %bitcast.6, bf16[4,128,256]{2,1,0:T(8,128)(2,1)} %bitcast.8, s32[16,27]{1,0:T(8,128)} %bitcast.9, s32[1,1]{1,0:T(1,128)S(6)} %copy.7.counts_ref, bf16[27,256,256]{2,1,0:T(8,128)(2,1)} %weight_hbm.1), custom_call_target="tpu_custom_call" | custom-call | flops 14499999744 | bytes 8000000 | tf_op jit(solution)/shard_map/pallas_call | solution.py:372
  48.6 1.0 %shard_map.69 = (bf16[16,128,256]{2,1,0:T(8,128)(2,1)}, f32[54,256]{1,0:T(8,128)}) custom-call(bf16[16,128,256]{2,1,0:T(8,128)(2,1)S(1)} %get-tuple-element.6.fine_in, f32[54,256]{1,0:T(8,128)S(1)} %get-tuple-element.7.weight_in), custom_call_target="tpu_custom_call" | custom-call | tf_op jit(solution)/shard_map/pallas_call | solution.py:404

commit v4 on v3

--- a/solution.py
+++ b/solution.py
@@ -197,19 +197,19 @@
             total = piece if total is None else total + piece
         return total * (1.0 / math.sqrt(262144))
 
-    def first_half(g, carry):
-        for i in range(9):
-            k = 9 * g + i
-            total = weight_offset(k, 0)
-            for side in range(2):
-                acc[side, pl.ds(pl.multiple_of(k * C, C), C), :] = total[:, side * HALF : (side + 1) * HALF]
-        return carry
-
     begin = (gx + 1) % 4
     begin = jnp.where(begin == 0, 0, jnp.where(begin == 1, 6, jnp.where(begin == 2, 13, 20)))
 
     def rows_of(n):
         return pl.ds(pl.multiple_of((begin + n) % K * C, C), C)
+
+    def first_half(g, carry):
+        for i in range(7):
+            n = 7 * g + i
+            total = weight_offset((begin + n) % K, 0)
+            for side in range(2):
+                acc[side, rows_of(n), :] = total[:, side * HALF : (side + 1) * HALF]
+        return carry
 
     def mate_copy(n):
         rows = rows_of(n)
@@ -221,8 +221,11 @@
     def weight_group(start, end):
         for n in range(start, end):
             total = weight_offset((begin + n) % K, 1)
+            if n >= 21:
+                total = total + weight_offset((begin + n) % K, 0)
             for side in range(2):
-                acc[side, rows_of(n), :] += total[:, side * HALF : (side + 1) * HALF]
+                piece = total[:, side * HALF : (side + 1) * HALF]
+                acc[side, rows_of(n), :] = piece if n >= 21 else acc[side, rows_of(n), :] + piece
         for n in range(start, end):
             mate_copy(n).start()
 
@@ -310,12 +313,26 @@
     fine_step(2)
     second_stage(1)
     fine_step(3)
+    second_stage(2)
     fine_step(4)
-    second_stage(2)
     fine_step(5)
+    second_stage(3)
     fine_step(6)
-    second_stage(3)
     fine_step(7)
+
+    for h, j in ORDER:
+        for i in range(2):
+            x_copy(i, h, j).wait_send()
+            y_copy(i, 1, h, j).wait_send()
+
+    def drain_mate(n, carry):
+        mate_copy(n).wait_send()
+        return carry
+
+    lax.fori_loop(0, K, drain_mate, 0)
+    for g in range(4):
+        for s in (1, 2, 3):
+            first_copy(g, s).wait_send()
 
     summed = total2[...]
     for e in range(3):
@@ -330,19 +347,7 @@
     last.wait_recv()
     weight_out[:, pl.ds(pl.multiple_of((1 - c) * HALF, HALF), HALF)] = mate_rows[0:MINE, :]
 
-    for h, j in ORDER:
-        for i in range(2):
-            x_copy(i, h, j).wait_send()
-            y_copy(i, 1, h, j).wait_send()
-
-    def drain_mate(n, carry):
-        mate_copy(n).wait_send()
-        return carry
-
-    lax.fori_loop(0, K, drain_mate, 0)
     for g in range(4):
-        for s in (1, 2, 3):
-            first_copy(g, s).wait_send()
         if g < 3:
             second_copy(g).wait_send()
 

time: 49.8 us -> 48.9 us (0.982)
  Pallas kernels: 48.3 us -> 47.5 us
    pallas_call x1, Pallas kernels: 47.3 us -> 46.5 us  [local(): pl.pallas_call(kernel, out_shape=(pltpu.VMEM((SLOTS, BLOCK, C), BF16), pl...]
where the time goes in v4:
time: 48.9 us; the launch traced here: 48.8 us
  Pallas kernels  47.5 us (97%)
  between operations  1.28 us (3%)
    pallas_call x1, Pallas kernels, local(): pl.pallas_call(kernel, out_shape=(pltpu.VMEM((SLOTS, BLOCK, C), BF16), pl...  46.5 us
    pallas_call x1, Pallas kernels, local(): pl.pallas_call(finish, out_shape=(jax.ShapeDtypeStruct((SLOTS, BLOCK, C),...  1.02 us

profile of v4, /device:TPU:1, one launch (start us, length us, event | category | flops | bytes accessed | tf_op | source)
XLA Modules:
  0.0 48.8 jit_solution(12523778835178550479)
XLA Ops:
  1.3 46.5 %shard_map.68 = (bf16[16,128,256]{2,1,0:T(8,128)(2,1)S(1)}, f32[54,256]{1,0:T(8,128)S(1)}) custom-call(bf16[16,128,256]{2,1,0:T(8,128)(2,1)} %bitcast.6, bf16[4,128,256]{2,1,0:T(8,128)(2,1)} %bitcast.8, s32[16,27]{1,0:T(8,128)} %bitcast.9, s32[1,1]{1,0:T(1,128)S(6)} %copy.7.counts_ref, bf16[27,256,256]{2,1,0:T(8,128)(2,1)} %weight_hbm.1), custom_call_target="tpu_custom_call" | custom-call | flops 14499999744 | bytes 8000000 | tf_op jit(solution)/shard_map/pallas_call | solution.py:377
  47.7 1.0 %shard_map.69 = (bf16[16,128,256]{2,1,0:T(8,128)(2,1)}, f32[54,256]{1,0:T(8,128)}) custom-call(bf16[16,128,256]{2,1,0:T(8,128)(2,1)S(1)} %get-tuple-element.6.fine_in, f32[54,256]{1,0:T(8,128)S(1)} %get-tuple-element.7.weight_in), custom_call_target="tpu_custom_call" | custom-call | tf_op jit(solution)/shard_map/pallas_call | solution.py:409

commit v5 on v4

--- a/solution.py
+++ b/solution.py
@@ -173,16 +173,15 @@
         return carry
 
     forward(0, 0)
-    lax.fori_loop(0, 9, turn, 0)
     forward(0, 1)
     own_along_y(1, 0)
     for i in range(2):
         y_copy(i, 1, 1, 1).wait_recv()
     for p in (0, 2):
         corner_copy(p).start()
-    lax.fori_loop(9, 18, turn, 0)
+    lax.fori_loop(0, 14, turn, 0)
     forward(1, 0)
-    lax.fori_loop(18, K, turn, 0)
+    lax.fori_loop(14, K, turn, 0)
     forward(1, 1)
     halo_done(0)
 

time: 48.9 us -> 48.8 us (level)
  no operation moved by 1% of the time
where the time goes in v5:
time: 48.8 us; the launch traced here: 48.7 us
  Pallas kernels  47.4 us (97%)
  between operations  1.28 us (3%)
    pallas_call x1, Pallas kernels, local(): pl.pallas_call(kernel, out_shape=(pltpu.VMEM((SLOTS, BLOCK, C), BF16), pl...  46.4 us
    pallas_call x1, Pallas kernels, local(): pl.pallas_call(finish, out_shape=(jax.ShapeDtypeStruct((SLOTS, BLOCK, C),...  1.02 us

profile of v5, /device:TPU:1, one launch (start us, length us, event | category | flops | bytes accessed | tf_op | source)
XLA Modules:
  0.0 48.7 jit_solution(7205036570781568203)
XLA Ops:
  1.3 46.4 %shard_map.68 = (bf16[16,128,256]{2,1,0:T(8,128)(2,1)S(1)}, f32[54,256]{1,0:T(8,128)S(1)}) custom-call(bf16[16,128,256]{2,1,0:T(8,128)(2,1)} %bitcast.6, bf16[4,128,256]{2,1,0:T(8,128)(2,1)} %bitcast.8, s32[16,27]{1,0:T(8,128)} %bitcast.9, s32[1,1]{1,0:T(1,128)S(6)} %copy.7.counts_ref, bf16[27,256,256]{2,1,0:T(8,128)(2,1)} %weight_hbm.1), custom_call_target="tpu_custom_call" | custom-call | flops 14499999744 | bytes 8000000 | tf_op jit(solution)/shard_map/pallas_call | solution.py:376
  47.7 1.0 %shard_map.69 = (bf16[16,128,256]{2,1,0:T(8,128)(2,1)}, f32[54,256]{1,0:T(8,128)}) custom-call(bf16[16,128,256]{2,1,0:T(8,128)(2,1)S(1)} %get-tuple-element.6.fine_in, f32[54,256]{1,0:T(8,128)S(1)} %get-tuple-element.7.weight_in), custom_call_target="tpu_custom_call" | custom-call | tf_op jit(solution)/shard_map/pallas_call | solution.py:408

commit v6 on v5

--- a/solution.py
+++ b/solution.py
@@ -292,7 +292,7 @@
             )
 
     def fine_step(s):
-        fine_part(s, 2)
+        fine_part(s, 4)
 
 
     lax.fori_loop(0, 3, first_half, 0)
@@ -309,15 +309,11 @@
     first_stage(3)
     second_stage(0)
     fine_step(1)
+    second_stage(1)
+    second_stage(2)
     fine_step(2)
-    second_stage(1)
+    second_stage(3)
     fine_step(3)
-    second_stage(2)
-    fine_step(4)
-    fine_step(5)
-    second_stage(3)
-    fine_step(6)
-    fine_step(7)
 
     for h, j in ORDER:
         for i in range(2):

time: 48.8 us -> 53.1 us (1.088)
  Pallas kernels: 47.4 us -> 51.7 us
    pallas_call x1, Pallas kernels: 46.4 us -> 50.7 us  [local(): pl.pallas_call(kernel, out_shape=(pltpu.VMEM((SLOTS, BLOCK, C), BF16), pl...]
where the time goes in v6:
time: 53.1 us; the launch traced here: 53 us
  Pallas kernels  51.7 us (97%)
  between operations  1.28 us (2%)
    pallas_call x1, Pallas kernels, local(): pl.pallas_call(kernel, out_shape=(pltpu.VMEM((SLOTS, BLOCK, C), BF16), pl...  50.7 us

profile of v6, /device:TPU:1, one launch (start us, length us, event | category | flops | bytes accessed | tf_op | source)
XLA Modules:
  0.0 53.0 jit_solution(13849389933579383638)
XLA Ops:
  1.3 50.7 %shard_map.68 = (bf16[16,128,256]{2,1,0:T(8,128)(2,1)S(1)}, f32[54,256]{1,0:T(8,128)S(1)}) custom-call(bf16[16,128,256]{2,1,0:T(8,128)(2,1)} %bitcast.6, bf16[4,128,256]{2,1,0:T(8,128)(2,1)} %bitcast.8, s32[16,27]{1,0:T(8,128)} %bitcast.9, s32[1,1]{1,0:T(1,128)S(6)} %copy.7.counts_ref, bf16[27,256,256]{2,1,0:T(8,128)(2,1)} %weight_hbm.1), custom_call_target="tpu_custom_call" | custom-call | flops 14499999744 | bytes 8000000 | tf_op jit(solution)/shard_map/pallas_call | solution.py:372
  51.9 1.0 %shard_map.69 = (bf16[16,128,256]{2,1,0:T(8,128)(2,1)}, f32[54,256]{1,0:T(8,128)}) custom-call(bf16[16,128,256]{2,1,0:T(8,128)(2,1)S(1)} %get-tuple-element.6.fine_in, f32[54,256]{1,0:T(8,128)S(1)} %get-tuple-element.7.weight_in), custom_call_target="tpu_custom_call" | custom-call | tf_op jit(solution)/shard_map/pallas_call | solution.py:404
